TPU v7x, 32 devices: a whole 2x2x4 slice. The times are simulated.
32 devices in a mesh: col: 4 (over y, x), gz: 8 (over z, core).
Axes of the slice: x: 2, y: 2, z: 4, core: 2. Of those that a mesh axis runs over, the one named last changes fastest.
Arguments:
- segments: float32 [9, 98304], P(None, ('col', 'gz')), may hold values from -6 to 6
- node_owner: int32 [2, 98304], P(None, ('col', 'gz')), may hold values from 0 to 4
- node_slot: int32 [2, 98304], P(None, ('col', 'gz')), may hold values from 0 to 3071
- pair_first: int32 [10240], P(('col', 'gz')), may hold values from 0 to 23
- pair_second: int32 [10240], P(('col', 'gz')), may hold values from 0 to 71
- pair_count: int32 [32], P(('col', 'gz')), may hold values from 106 to 320, as said below
Outputs:
- node_force: float32 [3, 98304], P(None, ('col', 'gz'))
Inputs may be any that keep to these rules, and one draw needn't show every extreme that they name: `pair_count`: each device has at least 106 listed pairs (a third, rounded down), and some device has exactly 320; entries past a device's count are ignored.
All inputs are finite; a program needn't handle non-finite values.
Results may differ from a plain program's by a relative error of at most 0.0003.
Values sent between devices are 32-bit elements; how exact they have to be, the bound alone decides.
No kernel may reach another device: no remote copies, remote signals or barrier semaphores. Data moves between devices by JAX's collectives and lax.ppermute only.
A program may use at most 64 MiB of HBM per device.

v0:
```python
import functools

import jax
import jax.numpy as jnp
from jax import lax
from jax.experimental import pallas as pl
from jax.experimental.pallas import tpu as pltpu
from jax.sharding import PartitionSpec as P

BLK = 128
NODE_DEV = 3072
MU = 0.02
CORE_SQ = 0.5

ROWS = 64
MOM = 16
GROUPS = (128, 64, 32, 16)
WIDE = 256
EARLY = 64
AHEAD = 16
BF = jnp.bfloat16
F32 = jnp.float32

_TN = (((0,), (0,)), ((), ()))
_NT = (((1,), (1,)), ((), ()))


def split3(v):
    a = v.astype(BF).astype(F32)
    r = v - a
    b = r.astype(BF).astype(F32)
    return a, b, r - b


def gather_components(seg_ref, comp, blocks):
    for b in range(blocks):
        lanes = slice(b * BLK, (b + 1) * BLK)
        comp[pl.ds(b, 8, stride=blocks), :] = seg_ref[0:8, lanes]
        comp[8 * blocks + b : 8 * blocks + b + 1, :] = seg_ref[8:9, lanes]


def features(comp, blocks):
    part = [comp[c * blocks : (c + 1) * blocks, :] for c in range(9)]
    x, burgers, line = part[0:3], part[3:6], part[6:9]
    xs = [split3(v) for v in x]
    norm = x[0] * x[0] + x[1] * x[1] + x[2] * x[2]
    prods = [split3(p * q)[0:1] + (p * q,) for p in burgers for q in line]
    prods = [(hi, full - hi) for hi, full in prods]
    return xs, norm, prods


def source_rows(xs, norm, prods):
    one = jnp.ones_like(norm)
    rows = {}
    norms = split3(norm + CORE_SQ)
    for k in range(3):
        x1, x2, x3 = xs[k]
        rows[k], rows[3 + k], rows[6 + k] = x1, x2, x3
        rows[9 + k], rows[12 + k] = one, norms[k]
        rows[15 + k], rows[18 + k], rows[21 + k] = x1, x2, x1
    for m, (hi, lo) in enumerate(prods):
        rows[32 + m], rows[41 + m], rows[50 + m] = hi, lo, hi
    return rows


def target_rows(xs, norm, prods):
    one = jnp.ones_like(norm)
    rows = {}
    norms = split3(norm)
    for k in range(3):
        x1, x2, x3 = (-2.0 * v for v in xs[k])
        rows[k], rows[3 + k], rows[6 + k] = x1, x1, x1
        rows[9 + k], rows[12 + k] = norms[k], one
        rows[15 + k], rows[18 + k], rows[21 + k] = x2, x2, x3
    for m, (hi, lo) in enumerate(prods):
        rows[32 + m], rows[41 + m], rows[50 + m] = hi, hi, lo
    return rows


def put_rows(rows, feat, blocks):
    for r in range(ROWS):
        feat[r * blocks : (r + 1) * blocks, :] = rows.get(r, jnp.zeros((blocks, BLK), F32))


def block_rows(feat, b, blocks):
    return feat[pl.ds(b, ROWS, stride=blocks), :].astype(BF)


def source_table(comp, feat, table, base, blocks):
    put_rows(source_rows(*features(comp, blocks)), feat, blocks)
    for b in range(blocks):
        table[base + b] = block_rows(feat, b, blocks)


def empty_block(table, at):
    row = lax.broadcasted_iota(jnp.int32, (ROWS, BLK), 0)
    table[at] = jnp.where(row == 12, 1.0, 0.0).astype(BF)


def pair_group(count, start, entry, target, source, forces):
    codes = [entry(start + u) for u in range(count)]

    def products(c):
        return lax.dot_general(source[c & 127], target[c >> 7], _TN, preferred_element_type=F32)

    ahead = {u: products(codes[u]) for u in range(min(AHEAD, count))}
    for u, c in enumerate(codes):
        if u + AHEAD < count:
            ahead[u + AHEAD] = products(codes[u + AHEAD])
        value = ahead.pop(u)
        inverse = lax.rsqrt(value[:, :BLK])
        coupling = value[:, BLK:] * inverse * (inverse * inverse)
        hi = coupling.astype(BF)
        lo = (coupling - hi.astype(F32)).astype(BF)
        moment = source[c & 127, 0:MOM, :]
        moment = jnp.concatenate([moment, moment], axis=1)
        weight = jnp.concatenate([hi, lo], axis=0)
        forces[c >> 7] += jnp.dot(moment, weight, preferred_element_type=F32)


def all_pairs(total, entry, target, source, forces, groups=GROUPS):
    whole = (total + (groups[-1] - 1)) // groups[0]

    def step(q, carry):
        pair_group(groups[0], q * groups[0], entry, target, source, forces)
        return carry

    lax.fori_loop(0, whole, step, 0)
    at = whole * groups[0]
    for count in groups[1:]:
        wanted = total > at + (count - groups[-1] if count > groups[-1] else 0)

        @pl.when(wanted)
        def _(count=count, at=at):
            pair_group(count, at, entry, target, source, forces)

        at = at + jnp.where(wanted, count, 0)


def sort_pairs(blocks, packed, lists):
    slots, places = packed.shape[1], lists.shape[1]
    listed = packed >= 0
    first, second = packed >> 7, packed & 127
    own = jnp.where(jnp.logical_and(listed, second < blocks), 1.0, 0.0)
    near = jnp.where(jnp.logical_and(listed, second < 2 * blocks), 1.0, 0.0)
    far = jnp.where(listed, 1.0, 0.0) - near
    line = lax.broadcasted_iota(jnp.int32, (16, slots), 0)
    member = jnp.where(line == 0, near - own, jnp.where(line == 1, far, jnp.where(line == 2, own, 0.0))).astype(BF)
    before = lax.broadcasted_iota(jnp.int32, (slots, slots), 0) < lax.broadcasted_iota(jnp.int32, (slots, slots), 1)
    rank = jnp.dot(member, jnp.where(before, 1.0, 0.0).astype(BF), preferred_element_type=F32)
    source = second - jnp.where(second >= 2 * blocks, 2 * blocks, 0)
    value = jnp.where(line == 0, first, jnp.where(line == 1, source, 0)).astype(F32).astype(BF)
    place = lax.broadcasted_iota(jnp.int32, (places, slots), 0).astype(F32)
    owned = jnp.sum(own, axis=1, keepdims=True)
    first_rank = jnp.where(own > 0.0, rank[2:3], rank[0:1] + owned)
    for r, (mine, ranks, empty) in enumerate(((near, first_rank, 2 * blocks), (far, rank[1:2], blocks))):
        at = jnp.where(mine > 0.0, ranks, -1.0)
        hit = jnp.where(place == at, 1.0, 0.0).astype(BF)
        found = lax.dot_general(value, hit, _NT, preferred_element_type=F32)
        code = (found[0:1] * 128.0 + found[1:2]).astype(jnp.int32)
        total = jnp.sum(mine, axis=1, keepdims=True).astype(jnp.int32)
        lane = lax.broadcasted_iota(jnp.int32, (1, places), 1)
        lists[r : r + 1, :] = jnp.where(lane < total, code, empty)
        lists[2 + r : 3 + r, :] = jnp.broadcast_to(total, (1, places))
    lists[4:5, :] = jnp.broadcast_to(owned.astype(jnp.int32), (1, places))


def own_tables(blocks, comp, feat, source, target):
    parts = features(comp, blocks)
    put_rows(source_rows(*parts), feat, blocks)
    for b in range(blocks):
        source[b] = block_rows(feat, b, blocks)
    xs, norm, prods = parts
    part = [comp[c * blocks : (c + 1) * blocks, :] for c in range(3, 9)]
    scaled = [MU * p * q for p in part[0:3] for q in part[3:6]]
    scaled = [(split3(v)[0], v) for v in scaled]
    scaled = [(hi, full - hi) for hi, full in scaled]
    put_rows(target_rows(xs, norm, scaled), feat, blocks)
    blank = jnp.zeros((ROWS // 2, BLK), BF)
    for b in range(blocks):
        rows = block_rows(feat, b, blocks)
        target[b, 0:32, 0:BLK] = rows[0:32]
        target[b, 0:32, BLK:] = blank
        target[b, 32:64, 0:BLK] = blank
        target[b, 32:64, BLK:] = rows[32:64]


def early_pairs(lists_ref):
    return jnp.minimum(lists_ref[4, 0] // GROUPS[-1] * GROUPS[-1], EARLY)


def first_kernel(
    blocks, packed_ref, seg_ref,
    lists, forces, source, target, comp,
    feat, counted, done,
):
    gather_components(seg_ref, comp, blocks)

    @pl.when(lax.axis_index("gz") == 0)
    def _():
        sort_pairs(blocks, packed_ref[...].reshape(1, packed_ref.shape[0]), lists)
        copy = pltpu.make_async_copy(lists, counted, done)
        copy.start()
        own_tables(blocks, comp, feat, source, target)
        forces[...] = jnp.zeros_like(forces)
        copy.wait()
        all_pairs(early_pairs(counted), lambda p: counted[0, p], target, source, forces, GROUPS[1:])


def near_kernel(
    blocks, packed_ref, near_ref, own_comp, early_lists, early_forces, early_source, early_target,
    forces_ref, target_ref, lists_ref,
    comp, feat, source, lists, done,
):
    early = lax.axis_index("gz") == 0
    copy = pltpu.make_async_copy(lists, lists_ref, done)

    @pl.when(early)
    def _():
        lists[...] = early_lists[...]
        copy.start()
        forces_ref[...] = early_forces[...]
        target_ref[...] = early_target[...]
        source[0:blocks] = early_source[...]

    @pl.when(jnp.logical_not(early))
    def _():
        sort_pairs(blocks, packed_ref[...].reshape(1, packed_ref.shape[0]), lists)
        copy.start()
        own_tables(blocks, own_comp, feat, source, target_ref)
        forces_ref[...] = jnp.zeros_like(forces_ref)

    gather_components(near_ref, comp, blocks)
    source_table(comp, feat, source, blocks, blocks)
    empty_block(source, 2 * blocks)
    copy.wait()
    base = jnp.where(early, early_pairs(lists_ref), 0)
    all_pairs(lists_ref[2, 0] - base, lambda p: lists_ref[0, base + p], target_ref, source, forces_ref)


def one_hot(at, row):
    return jnp.where(at == row, jnp.ones((), BF), jnp.zeros((), BF))


def span_of(targets):
    return -(-targets * (NODE_DEV // WIDE) // 8) * 8


def far_kernel(
    blocks, steps, lists_ref, far_ref, target_ref, comp_ref, near_forces,
    owner_ref, slot_ref, *rest,
):
    targets = 1 + 2 * len(set(steps))
    outs, (feat, source, forces, scaled, total_low, total_high) = rest[:targets], rest[targets:]
    source_table(far_ref, feat, source, 0, blocks)
    empty_block(source, blocks)
    forces[...] = near_forces[...]
    all_pairs(lists_ref[3, 0], lambda p: lists_ref[1, p], target_ref, source, forces)

    flat = forces.reshape(blocks * MOM, BLK)
    row = [flat[pl.ds(m, blocks, stride=MOM), :] for m in range(10)]
    for k in range(3):
        pulled = row[k] + row[3 + k] + row[6 + k]
        half = 0.5 * (comp_ref[k * blocks : (k + 1) * blocks, :] * row[9] - pulled)
        hi = half.astype(BF).astype(F32)
        scaled[k * blocks : (k + 1) * blocks, :] = hi
        scaled[(3 + k) * blocks : (4 + k) * blocks, :] = half - hi

    highs = NODE_DEV // WIDE
    span = span_of(targets)
    codes = owner_ref[...]
    column = lax.axis_index("col")
    place = jnp.zeros_like(codes)
    for n, step in enumerate(steps):
        to = 1 + 2 * steps.index(step)
        odd = (column // step) % 2
        place = jnp.where(codes == 1 + 2 * n, to + odd, place)
        place = jnp.where(codes == 2 + 2 * n, to + 1 - odd, place)
    slot = slot_ref[...]
    high = place * highs + slot // WIDE
    low = slot % WIDE
    high, low = high.astype(F32).astype(BF), low.astype(F32).astype(BF)
    high_at = lax.broadcasted_iota(jnp.int32, (span, BLK), 0).astype(F32).astype(BF)
    low_at = lax.broadcasted_iota(jnp.int32, (WIDE, BLK), 0).astype(F32).astype(BF)
    summed = None
    for first in range(0, blocks, 4):
        lefts, rights = [], []
        for b in range(first, first + 4):
            lanes = slice(b * BLK, (b + 1) * BLK)
            values = [scaled[m * blocks + b : m * blocks + b + 1, :].astype(BF) for m in range(6)]
            for end in range(2):
                rights.append(one_hot(low_at, low[end : end + 1, lanes]))
                hit = one_hot(high_at, high[end : end + 1, lanes])
                lefts.append(jnp.concatenate([hit * value for value in values], axis=0))
        part = lax.dot_general(
            jnp.concatenate(lefts, axis=1), jnp.concatenate(rights, axis=1), _NT, preferred_element_type=F32
        )
        summed = part if summed is None else summed + part
    summed = summed[: 3 * span] + summed[3 * span :]
    for half, total in enumerate((total_low, total_high)):
        total[...] = summed[:, half * BLK : (half + 1) * BLK]
    for t, out in enumerate(outs):
        for h in range(highs):
            for half, total in enumerate((total_low, total_high)):
                out[:, h * WIDE + half * BLK : h * WIDE + (half + 1) * BLK] = total[pl.ds(t * highs + h, 3, stride=span), :]


def swaps(peers, step, late):
    firsts = [i for i in range(peers) if (i // step) % 2 == late]
    return [(i, (i + step) % peers) for i in firsts] + [((i + step) % peers, i) for i in firsts]


def on_device(segments, node_owner, node_slot, pair_first, pair_second, pair_count):
    width = segments.shape[1]
    blocks = width // BLK
    slots = pair_first.shape[0]
    places = -(-(slots + GROUPS[0]) // BLK) * BLK
    peers = lax.axis_size("gz")
    smem = pl.BlockSpec(memory_space=pltpu.SMEM)
    vmem = pl.BlockSpec(memory_space=pltpu.VMEM)
    params = pltpu.CompilerParams(vmem_limit_bytes=40 << 20)

    near = lax.ppermute(segments, "gz", swaps(peers, 1, 0))

    odd = lax.axis_index("gz") % 2
    beyond = jnp.where(odd == 1, pair_second < blocks, pair_second >= 2 * blocks)
    own = jnp.logical_and(pair_second >= blocks, pair_second < 2 * blocks)
    region = jnp.where(own, 0, jnp.where(beyond, 1, 2))
    old = jnp.where(pair_second >= 2 * blocks, 2, jnp.where(pair_second >= blocks, 1, 0))
    renumbered = pair_second + (region - old) * blocks
    listed = jnp.arange(slots, dtype=jnp.int32) < pair_count[0]
    packed = jnp.where(listed, pair_first * 128 + renumbered, -1)

    early_shapes = (
        jax.ShapeDtypeStruct((8, places), jnp.int32),
        jax.ShapeDtypeStruct((blocks, MOM, BLK), F32),
        jax.ShapeDtypeStruct((blocks, ROWS, BLK), BF),
        jax.ShapeDtypeStruct((blocks, ROWS, 2 * BLK), BF),
        jax.ShapeDtypeStruct((9 * blocks, BLK), F32),
    )
    early = pl.pallas_call(
        functools.partial(first_kernel, blocks),
        out_shape=early_shapes,
        in_specs=[vmem, vmem],
        out_specs=(vmem,) * 5,
        scratch_shapes=[
            pltpu.VMEM((ROWS * blocks, BLK), F32),
            pltpu.SMEM((8, places), jnp.int32),
            pltpu.SemaphoreType.DMA,
        ],
        compiler_params=params,
    )(packed, segments)
    *early, comp = early
    far = lax.ppermute(comp, "gz", swaps(peers, 1, 1))

    forces, table, lists = pl.pallas_call(
        functools.partial(near_kernel, blocks),
        out_shape=(
            jax.ShapeDtypeStruct((blocks, MOM, BLK), F32),
            jax.ShapeDtypeStruct((blocks, ROWS, 2 * BLK), BF),
            jax.ShapeDtypeStruct((8, places), jnp.int32),
        ),
        in_specs=[vmem] * 7,
        out_specs=(vmem, vmem, smem),
        scratch_shapes=[
            pltpu.VMEM((9 * blocks, BLK), F32),
            pltpu.VMEM((ROWS * blocks, BLK), F32),
            pltpu.VMEM((2 * blocks + 1, ROWS, BLK), BF),
            pltpu.VMEM((8, places), jnp.int32),
            pltpu.SemaphoreType.DMA,
        ],
        compiler_params=params,
        cost_estimate=pl.CostEstimate(flops=10_000_000_000, bytes_accessed=1_000_000, transcendentals=0),
    )(packed, near, comp, *early)

    columns = lax.axis_size("col")
    steps = (1, columns // 4)
    distinct = list(dict.fromkeys(steps))
    targets = 1 + 2 * len(distinct)
    span = span_of(targets)
    partials = pl.pallas_call(
        functools.partial(far_kernel, blocks, steps),
        out_shape=tuple(jax.ShapeDtypeStruct((3, NODE_DEV), F32) for _ in range(targets)),
        in_specs=[smem] + [vmem] * 6,
        out_specs=(vmem,) * targets,
        scratch_shapes=[
            pltpu.VMEM((ROWS * blocks, BLK), F32),
            pltpu.VMEM((blocks + 1, ROWS, BLK), BF),
            pltpu.VMEM((blocks, MOM, BLK), F32),
            pltpu.VMEM((6 * blocks, BLK), F32),
            pltpu.VMEM((3 * span, BLK), F32),
            pltpu.VMEM((3 * span, BLK), F32),
        ],
        compiler_params=params,
    )(lists, far, table, comp, forces, node_owner, node_slot)
    node_total = partials[0]
    for n, partial in enumerate(partials[1:]):
        node_total = node_total + lax.ppermute(partial, "col", swaps(columns, distinct[n // 2], n % 2))
    return node_total


def solution(mesh):
    in_specs = (
        P(None, ("col", "gz")),
        P(None, ("col", "gz")),
        P(None, ("col", "gz")),
        P(("col", "gz")),
        P(("col", "gz")),
        P(("col", "gz")),
    )
    out_specs = P(None, ("col", "gz"))
    return jax.shard_map(
        on_device, mesh=mesh, in_specs=in_specs, out_specs=out_specs, check_vma=False
    )
```

profile of v0, /device:TPU:0, one launch (start us, length us, event | category | flops | bytes accessed | tf_op | source)
XLA Modules:
  0.0 23.9 jit_solution(14039781269324585724)
XLA Ops:
  0.0 0.5 %collective-permute-start = (f32[9,3072]{1,0:T(8,128)}, f32[9,3072]{1,0:T(8,128)S(1)}, u32[]{:S(2)}, u32[]{:S(2)}) collective-permute-start(f32[9,3072]{1,0:T(8,128)} %seg_ref.1), channel_id=1, source_target_pairs={{0,1},{2,3},{4,5},{6,7},{1,0},{3,2},{5,4},{7,6},{8,9},{10,11},{12,... | collective-permute-start | bytes 331784 | tf_op jit(solution)/shard_map/ppermute | solution.py:323
  0.5 0.0 copy-start.4
  0.5 0.0 copy-start.3
  1.1 0.0 copy-done.4
  1.1 0.0 copy-done.3
  1.2 0.0 copy-start
  1.2 0.9 %copy-done = f32[9,3072]{1,0:T(8,128)S(1)} copy-done((f32[9,3072]{1,0:T(8,128)S(1)}, f32[9,3072]{1,0:T(8,128)}, u32[]{:S(2)}) %copy-start) | copy-done | bytes 110616
  2.1 3.1 %shard_map.64 = (s32[8,512]{1,0:T(8,128)S(1)}, f32[24,16,128]{2,1,0:T(8,128)S(1)}, bf16[24,64,128]{2,1,0:T(8,128)(2,1)S(1)}, bf16[24,64,256]{2,1,0:T(8,128)(2,1)S(1)}, f32[216,128]{1,0:T(8,128)S(1)}) custom-call(s32[320]{0:T(512)S(1)} %add_select_fusion.packed_ref, f32[9,3072]{1,0:T(8,128)S(1)} %copy-done), custom_call_target="tpu_custom_call" | custom-call | tf_op jit(solution)/shard_map/pallas_call | solution.py:341
  5.2 1.7 %collective-permute-start.1 = (f32[216,128]{1,0:T(8,128)S(1)}, f32[216,128]{1,0:T(8,128)S(1)}, u32[]{:S(2)}, u32[]{:S(2)}) collective-permute-start(f32[216,128]{1,0:T(8,128)S(1)} %get-tuple-element.16.own_comp.comp_ref), channel_id=1, source_target_pairs={{1,2},{3,4},{5,6},{7,0},{2,1},{4,3},{6,5},{0,7},{9,10},{11,12},{13... | collective-permute-start | bytes 331784 | tf_op jit(solution)/shard_map/ppermute | solution.py:354
  6.9 0.0 collective-permute-done.near_ref
  6.9 0.0 copy-start.1
  6.9 0.0 copy-start.2
  6.9 5.8 %shard_map.65 = (f32[24,16,128]{2,1,0:T(8,128)S(1)}, bf16[24,64,256]{2,1,0:T(8,128)(2,1)S(1)}, s32[8,512]{1,0:T(8,128)S(1)}) custom-call(s32[320]{0:T(512)S(1)} %add_select_fusion.packed_ref, f32[9,3072]{1,0:T(8,128)S(1)} %collective-permute-done.near_ref, f32[216,128]{1,0:T(8,128)S(1)} %get-tuple-element.16.own_comp.comp_ref, ...), custom_call_target="tpu_custom_call" | custom-call | flops 10000000000 | bytes 1000000 | tf_op jit(solution)/shard_map/pallas_call | solution.py:356
  12.7 0.0 collective-permute-done.1.far_ref
  12.7 0.0 copy-done.1
  12.7 0.0 copy-done.2
  12.7 5.4 %shard_map.66 = (f32[3,3072]{1,0:T(4,128)S(1)}, f32[3,3072]{1,0:T(4,128)S(1)}, f32[3,3072]{1,0:T(4,128)S(1)}) custom-call(s32[8,512]{1,0:T(8,128)S(1)} %get-tuple-element.21.lists_ref, f32[216,128]{1,0:T(8,128)S(1)} %collective-permute-done.1.far_ref, bf16[24,64,256]{2,1,0:T(8,128)(2,1)S(1)} %get-tuple-element.22.target_ref, ...), custom_call_target="tpu_custom_call" | custom-call | tf_op jit(solution)/shard_map/pallas_call | solution.py:381
  18.2 0.1 collective-permute-start.2
  18.2 1.4 %collective-permute-start.3 = (f32[3,3072]{1,0:T(4,128)S(1)}, f32[3,3072]{1,0:T(4,128)S(1)}, u32[]{:S(2)}, u32[]{:S(2)}) collective-permute-start(f32[3,3072]{1,0:T(4,128)S(1)} %get-tuple-element.26), channel_id=1, source_target_pairs={{8,16},{24,0},{16,8},{0,24},{9,17},{25,1},{17,9},{1,25},{10,18},{2... | collective-permute-start | bytes 110600 | tf_op jit(solution)/shard_map/ppermute | solution.py:398
  19.7 2.9 %collective-permute-done.2 = f32[3,3072]{1,0:T(4,128)S(1)} collective-permute-done((f32[3,3072]{1,0:T(4,128)S(1)}, f32[3,3072]{1,0:T(4,128)S(1)}, u32[]{:S(2)}, u32[]{:S(2)}) %collective-permute-start.2) | collective-permute-done | bytes 36896 | tf_op jit(solution)/shard_map/ppermute | solution.py:398
  22.6 0.7 %collective-permute-done.3 = f32[3,3072]{1,0:T(4,128)S(1)} collective-permute-done((f32[3,3072]{1,0:T(4,128)S(1)}, f32[3,3072]{1,0:T(4,128)S(1)}, u32[]{:S(2)}, u32[]{:S(2)}) %collective-permute-start.3) | collective-permute-done | bytes 36896 | tf_op jit(solution)/shard_map/ppermute | solution.py:398
  23.3 0.6 %add_add_fusion = f32[3,3072]{1,0:T(4,128)} fusion(f32[3,3072]{1,0:T(4,128)S(1)} %collective-permute-done.3, f32[3,3072]{1,0:T(4,128)S(1)} %get-tuple-element.24, f32[3,3072]{1,0:T(4,128)S(1)} %collective-permute-done.2), kind=kLoop, calls=%fused_computation | loop fusion | flops 18432 | bytes 147456 | tf_op jit(solution)/shard_map/add | solution.py:398
  (1 shorter events, 0.0 us)
Async XLA Ops:
  0.0 6.9 %collective-permute-start = (f32[9,3072]{1,0:T(8,128)}, f32[9,3072]{1,0:T(8,128)S(1)}, u32[]{:S(2)}, u32[]{:S(2)}) collective-permute-start(f32[9,3072]{1,0:T(8,128)} %seg_ref.1), channel_id=1, source_target_pairs={{0,1},{2,3},{4,5},{6,7},{1,0},{3,2},{5,4},{7,6},{8,9},{10,11},{12,... | collective-permute-start | bytes 331784 | tf_op jit(solution)/shard_map/ppermute | solution.py:323
  0.5 0.7 %copy-start.4 = (s32[320]{0:T(512)S(1)}, s32[320]{0:T(512)}, u32[]{:S(2)}) copy-start(s32[320]{0:T(512)} %param.9) | copy-start | bytes 3844
  0.5 0.7 %copy-start.3 = (s32[320]{0:T(512)S(1)}, s32[320]{0:T(512)}, u32[]{:S(2)}) copy-start(s32[320]{0:T(512)} %param.10) | copy-start | bytes 3844
  1.2 0.9 %copy-start = (f32[9,3072]{1,0:T(8,128)S(1)}, f32[9,3072]{1,0:T(8,128)}, u32[]{:S(2)}) copy-start(f32[9,3072]{1,0:T(8,128)} %seg_ref.1) | copy-start | bytes 331780
  5.2 7.5 %collective-permute-start.1 = (f32[216,128]{1,0:T(8,128)S(1)}, f32[216,128]{1,0:T(8,128)S(1)}, u32[]{:S(2)}, u32[]{:S(2)}) collective-permute-start(f32[216,128]{1,0:T(8,128)S(1)} %get-tuple-element.16.own_comp.comp_ref), channel_id=1, source_target_pairs={{1,2},{3,4},{5,6},{7,0},{2,1},{4,3},{6,5},{0,7},{9,10},{11,12},{13... | collective-permute-start | bytes 331784 | tf_op jit(solution)/shard_map/ppermute | solution.py:354
  6.9 5.8 %copy-start.1 = (s32[2,3072]{1,0:T(2,128)S(1)}, s32[2,3072]{1,0:T(2,128)}, u32[]{:S(2)}) copy-start(s32[2,3072]{1,0:T(2,128)} %owner_ref.1) | copy-start | bytes 73732
  6.9 5.8 %copy-start.2 = (s32[2,3072]{1,0:T(2,128)S(1)}, s32[2,3072]{1,0:T(2,128)}, u32[]{:S(2)}) copy-start(s32[2,3072]{1,0:T(2,128)} %slot_ref.1) | copy-start | bytes 73732
  18.2 4.4 %collective-permute-start.2 = (f32[3,3072]{1,0:T(4,128)S(1)}, f32[3,3072]{1,0:T(4,128)S(1)}, u32[]{:S(2)}, u32[]{:S(2)}) collective-permute-start(f32[3,3072]{1,0:T(4,128)S(1)} %get-tuple-element.25), channel_id=1, source_target_pairs={{0,8},{16,24},{8,0},{24,16},{1,9},{17,25},{9,1},{25,17},{2,10},{18... | collective-permute-start | bytes 110600 | tf_op jit(solution)/shard_map/ppermute | solution.py:398
  18.2 5.1 %collective-permute-start.3 = (f32[3,3072]{1,0:T(4,128)S(1)}, f32[3,3072]{1,0:T(4,128)S(1)}, u32[]{:S(2)}, u32[]{:S(2)}) collective-permute-start(f32[3,3072]{1,0:T(4,128)S(1)} %get-tuple-element.26), channel_id=1, source_target_pairs={{8,16},{24,0},{16,8},{0,24},{9,17},{25,1},{17,9},{1,25},{10,18},{2... | collective-permute-start | bytes 110600 | tf_op jit(solution)/shard_map/ppermute | solution.py:398
where the time goes:
time: 24.2 us; the launch traced here: 23.9 us
  Pallas kernels  14.3 us (59%)
  starting transfers between devices  3.69 us (15%)
  waiting for transfers between devices  3.62 us (15%)
  local copies, waits for them, and re-layouts  0.94 us (4%)
  between operations  0.77 us (3%)
  other arithmetic  0.65 us (3%)
    pallas_call x1, Pallas kernels, on_device(): pl.pallas_call(functools.partial(near_kernel, blocks), out_shape=(jax.Sha...  5.75 us
    pallas_call x1, Pallas kernels, on_device(): pl.pallas_call(functools.partial(far_kernel, blocks, steps), out_shape=tu...  5.44 us
    ppermute x2, waiting for transfers between devices, on_device(): lax.ppermute(partial, 'col', swaps(columns, distinct[n // 2], n % 2))  3.61 us
    pallas_call x1, Pallas kernels, on_device(): pl.pallas_call(functools.partial(first_kernel, blocks), out_shape=early_s...  3.08 us
    ppermute x1, starting transfers between devices, on_device(): far = lax.ppermute(comp, 'gz', swaps(peers, 1, 1))  1.73 us
    ppermute x2, starting transfers between devices, on_device(): lax.ppermute(partial, 'col', swaps(columns, distinct[n // 2], n % 2))  1.51 us
    unnamed x10, local copies, waits for them, and re-layouts  0.94 us
    add x1, other arithmetic, on_device(): node_total + lax.ppermute(partial, 'col', swaps(columns, distinct[n // 2]...  0.64 us
  transfers between devices with their start and end apart: 4, of which 2 were waited for; matrix products, arithmetic and copies ran while one was open for 0% of the time, Pallas kernels for 37%

commit v1 on v0

--- a/solution.py
+++ b/solution.py
@@ -16,7 +16,7 @@
 MOM = 16
 GROUPS = (128, 64, 32, 16)
 WIDE = 256
-EARLY = 64
+EARLY = 32
 AHEAD = 16
 BF = jnp.bfloat16
 F32 = jnp.float32
@@ -204,7 +204,7 @@
         own_tables(blocks, comp, feat, source, target)
         forces[...] = jnp.zeros_like(forces)
         copy.wait()
-        all_pairs(early_pairs(counted), lambda p: counted[0, p], target, source, forces, GROUPS[1:])
+        all_pairs(early_pairs(counted), lambda p: counted[0, p], target, source, forces, GROUPS[2:])
 
 
 def near_kernel(

time: 24.2 us -> 25 us (1.033)
  starting transfers between devices: 3.69 us -> 9.16 us
  Pallas kernels: 14.3 us -> 10.2 us
  waiting for transfers between devices: 3.62 us -> 2.91 us
    ppermute x2, starting transfers between devices: 1.51 us -> 6.27 us  [on_device(): lax.ppermute(partial, 'col', swaps(columns, distinct[n // 2], n % 2))]
    pallas_call x1, Pallas kernels: 5.75 us -> 3.98 us  [on_device(): pl.pallas_call(functools.partial(near_kernel, blocks), out_shape=(jax.Sha...]
    pallas_call x1, Pallas kernels: 5.44 us -> 3.8 us  [on_device(): pl.pallas_call(functools.partial(far_kernel, blocks, steps), out_shape=tu...]
    ppermute x2, waiting for transfers between devices: 3.61 us -> 2.55 us  [on_device(): lax.ppermute(partial, 'col', swaps(columns, distinct[n // 2], n % 2))]
    ppermute x1, starting transfers between devices: 1.73 us -> 2.44 us  [on_device(): far = lax.ppermute(comp, 'gz', swaps(peers, 1, 1))]
    pallas_call x1, Pallas kernels: 3.08 us -> 2.37 us  [on_device(): pl.pallas_call(functools.partial(first_kernel, blocks), out_shape=early_s...]
    ppermute x1, waiting for transfers between devices: 0.01 us -> 0.36 us  [on_device(): far = lax.ppermute(comp, 'gz', swaps(peers, 1, 1))]
  transfers between devices with their start and end apart: 4 -> 4, of which waited for: 2 -> 2; matrix products, arithmetic and copies ran while one was open for 0% -> 0% of each run, Pallas kernels for 37% -> 26%
where the time goes in v1:
time: 25 us; the launch traced here: 24.6 us
  Pallas kernels  10.2 us (41%)
  starting transfers between devices  9.16 us (37%)
  waiting for transfers between devices  2.91 us (12%)
  local copies, waits for them, and re-layouts  0.94 us (4%)
  between operations  0.74 us (3%)
  other arithmetic  0.65 us (3%)
    ppermute x2, starting transfers between devices, on_device(): lax.ppermute(partial, 'col', swaps(columns, distinct[n // 2], n % 2))  6.27 us
    pallas_call x1, Pallas kernels, on_device(): pl.pallas_call(functools.partial(near_kernel, blocks), out_shape=(jax.Sha...  3.98 us
    pallas_call x1, Pallas kernels, on_device(): pl.pallas_call(functools.partial(far_kernel, blocks, steps), out_shape=tu...  3.8 us
    ppermute x2, waiting for transfers between devices, on_device(): lax.ppermute(partial, 'col', swaps(columns, distinct[n // 2], n % 2))  2.55 us
    ppermute x1, starting transfers between devices, on_device(): far = lax.ppermute(comp, 'gz', swaps(peers, 1, 1))  2.44 us
    pallas_call x1, Pallas kernels, on_device(): pl.pallas_call(functools.partial(first_kernel, blocks), out_shape=early_s...  2.37 us
    unnamed x10, local copies, waits for them, and re-layouts  0.94 us
    add x1, other arithmetic, on_device(): node_total + lax.ppermute(partial, 'col', swaps(columns, distinct[n // 2]...  0.64 us
  transfers between devices with their start and end apart: 4, of which 2 were waited for; matrix products, arithmetic and copies ran while one was open for 0% of the time, Pallas kernels for 26%

profile of v1, /device:TPU:0, one launch (start us, length us, event | category | flops | bytes accessed | tf_op | source)
XLA Modules:
  0.0 24.6 jit_solution(4478436916828279065)
XLA Ops:
  0.0 0.5 %collective-permute-start = (f32[9,3072]{1,0:T(8,128)}, f32[9,3072]{1,0:T(8,128)S(1)}, u32[]{:S(2)}, u32[]{:S(2)}) collective-permute-start(f32[9,3072]{1,0:T(8,128)} %seg_ref.1), channel_id=1, source_target_pairs={{0,1},{2,3},{4,5},{6,7},{1,0},{3,2},{5,4},{7,6},{8,9},{10,11},{12,... | collective-permute-start | bytes 331784 | tf_op jit(solution)/shard_map/ppermute | solution.py:323
  0.5 0.0 copy-start.4
  0.5 0.0 copy-start.3
  1.1 0.0 copy-done.4
  1.1 0.0 copy-done.3
  1.2 0.0 copy-start
  1.2 0.9 %copy-done = f32[9,3072]{1,0:T(8,128)S(1)} copy-done((f32[9,3072]{1,0:T(8,128)S(1)}, f32[9,3072]{1,0:T(8,128)}, u32[]{:S(2)}) %copy-start) | copy-done | bytes 110616
  2.1 2.4 %shard_map.64 = (s32[8,512]{1,0:T(8,128)S(1)}, f32[24,16,128]{2,1,0:T(8,128)S(1)}, bf16[24,64,128]{2,1,0:T(8,128)(2,1)S(1)}, bf16[24,64,256]{2,1,0:T(8,128)(2,1)S(1)}, f32[216,128]{1,0:T(8,128)S(1)}) custom-call(s32[320]{0:T(512)S(1)} %add_select_fusion.packed_ref, f32[9,3072]{1,0:T(8,128)S(1)} %copy-done), custom_call_target="tpu_custom_call" | custom-call | tf_op jit(solution)/shard_map/pallas_call | solution.py:341
  4.5 2.4 %collective-permute-start.1 = (f32[216,128]{1,0:T(8,128)S(1)}, f32[216,128]{1,0:T(8,128)S(1)}, u32[]{:S(2)}, u32[]{:S(2)}) collective-permute-start(f32[216,128]{1,0:T(8,128)S(1)} %get-tuple-element.16.own_comp.comp_ref), channel_id=1, source_target_pairs={{1,2},{3,4},{5,6},{7,0},{2,1},{4,3},{6,5},{0,7},{9,10},{11,12},{13... | collective-permute-start | bytes 331784 | tf_op jit(solution)/shard_map/ppermute | solution.py:354
  6.9 0.0 collective-permute-done.near_ref
  6.9 0.0 copy-start.1
  6.9 0.0 copy-start.2
  6.9 4.0 %shard_map.65 = (f32[24,16,128]{2,1,0:T(8,128)S(1)}, bf16[24,64,256]{2,1,0:T(8,128)(2,1)S(1)}, s32[8,512]{1,0:T(8,128)S(1)}) custom-call(s32[320]{0:T(512)S(1)} %add_select_fusion.packed_ref, f32[9,3072]{1,0:T(8,128)S(1)} %collective-permute-done.near_ref, f32[216,128]{1,0:T(8,128)S(1)} %get-tuple-element.16.own_comp.comp_ref, ...), custom_call_target="tpu_custom_call" | custom-call | flops 10000000000 | bytes 1000000 | tf_op jit(solution)/shard_map/pallas_call | solution.py:356
  10.9 0.4 %collective-permute-done.1.far_ref = f32[216,128]{1,0:T(8,128)S(1)} collective-permute-done((f32[216,128]{1,0:T(8,128)S(1)}, f32[216,128]{1,0:T(8,128)S(1)}, u32[]{:S(2)}, u32[]{:S(2)}) %collective-permute-start.1) | collective-permute-done | bytes 110624 | tf_op jit(solution)/shard_map/ppermute | solution.py:354
  11.3 0.0 copy-done.1
  11.3 0.0 copy-done.2
  11.3 3.8 %shard_map.66 = (f32[3,3072]{1,0:T(4,128)S(1)}, f32[3,3072]{1,0:T(4,128)S(1)}, f32[3,3072]{1,0:T(4,128)S(1)}) custom-call(s32[8,512]{1,0:T(8,128)S(1)} %get-tuple-element.21.lists_ref, f32[216,128]{1,0:T(8,128)S(1)} %collective-permute-done.1.far_ref, bf16[24,64,256]{2,1,0:T(8,128)(2,1)S(1)} %get-tuple-element.22.target_ref, ...), custom_call_target="tpu_custom_call" | custom-call | tf_op jit(solution)/shard_map/pallas_call | solution.py:381
  15.1 1.9 %collective-permute-start.2 = (f32[3,3072]{1,0:T(4,128)S(1)}, f32[3,3072]{1,0:T(4,128)S(1)}, u32[]{:S(2)}, u32[]{:S(2)}) collective-permute-start(f32[3,3072]{1,0:T(4,128)S(1)} %get-tuple-element.25), channel_id=1, source_target_pairs={{0,8},{16,24},{8,0},{24,16},{1,9},{17,25},{9,1},{25,17},{2,10},{18... | collective-permute-start | bytes 110600 | tf_op jit(solution)/shard_map/ppermute | solution.py:398
  17.0 4.4 %collective-permute-start.3 = (f32[3,3072]{1,0:T(4,128)S(1)}, f32[3,3072]{1,0:T(4,128)S(1)}, u32[]{:S(2)}, u32[]{:S(2)}) collective-permute-start(f32[3,3072]{1,0:T(4,128)S(1)} %get-tuple-element.26), channel_id=1, source_target_pairs={{8,16},{24,0},{16,8},{0,24},{9,17},{25,1},{17,9},{1,25},{10,18},{2... | collective-permute-start | bytes 110600 | tf_op jit(solution)/shard_map/ppermute | solution.py:398
  21.4 0.0 collective-permute-done.2
  21.4 2.5 %collective-permute-done.3 = f32[3,3072]{1,0:T(4,128)S(1)} collective-permute-done((f32[3,3072]{1,0:T(4,128)S(1)}, f32[3,3072]{1,0:T(4,128)S(1)}, u32[]{:S(2)}, u32[]{:S(2)}) %collective-permute-start.3) | collective-permute-done | bytes 36896 | tf_op jit(solution)/shard_map/ppermute | solution.py:398
  23.9 0.6 %add_add_fusion = f32[3,3072]{1,0:T(4,128)} fusion(f32[3,3072]{1,0:T(4,128)S(1)} %collective-permute-done.3, f32[3,3072]{1,0:T(4,128)S(1)} %get-tuple-element.24, f32[3,3072]{1,0:T(4,128)S(1)} %collective-permute-done.2), kind=kLoop, calls=%fused_computation | loop fusion | flops 18432 | bytes 147456 | tf_op jit(solution)/shard_map/add | solution.py:398
  (1 shorter events, 0.0 us)
Async XLA Ops:
  0.0 6.9 %collective-permute-start = (f32[9,3072]{1,0:T(8,128)}, f32[9,3072]{1,0:T(8,128)S(1)}, u32[]{:S(2)}, u32[]{:S(2)}) collective-permute-start(f32[9,3072]{1,0:T(8,128)} %seg_ref.1), channel_id=1, source_target_pairs={{0,1},{2,3},{4,5},{6,7},{1,0},{3,2},{5,4},{7,6},{8,9},{10,11},{12,... | collective-permute-start | bytes 331784 | tf_op jit(solution)/shard_map/ppermute | solution.py:323
  0.5 0.7 %copy-start.4 = (s32[320]{0:T(512)S(1)}, s32[320]{0:T(512)}, u32[]{:S(2)}) copy-start(s32[320]{0:T(512)} %param.9) | copy-start | bytes 3844
  0.5 0.7 %copy-start.3 = (s32[320]{0:T(512)S(1)}, s32[320]{0:T(512)}, u32[]{:S(2)}) copy-start(s32[320]{0:T(512)} %param.10) | copy-start | bytes 3844
  1.2 0.9 %copy-start = (f32[9,3072]{1,0:T(8,128)S(1)}, f32[9,3072]{1,0:T(8,128)}, u32[]{:S(2)}) copy-start(f32[9,3072]{1,0:T(8,128)} %seg_ref.1) | copy-start | bytes 331780
  4.5 6.8 %collective-permute-start.1 = (f32[216,128]{1,0:T(8,128)S(1)}, f32[216,128]{1,0:T(8,128)S(1)}, u32[]{:S(2)}, u32[]{:S(2)}) collective-permute-start(f32[216,128]{1,0:T(8,128)S(1)} %get-tuple-element.16.own_comp.comp_ref), channel_id=1, source_target_pairs={{1,2},{3,4},{5,6},{7,0},{2,1},{4,3},{6,5},{0,7},{9,10},{11,12},{13... | collective-permute-start | bytes 331784 | tf_op jit(solution)/shard_map/ppermute | solution.py:354
  6.9 4.4 %copy-start.1 = (s32[2,3072]{1,0:T(2,128)S(1)}, s32[2,3072]{1,0:T(2,128)}, u32[]{:S(2)}) copy-start(s32[2,3072]{1,0:T(2,128)} %owner_ref.1) | copy-start | bytes 73732
  6.9 4.4 %copy-start.2 = (s32[2,3072]{1,0:T(2,128)S(1)}, s32[2,3072]{1,0:T(2,128)}, u32[]{:S(2)}) copy-start(s32[2,3072]{1,0:T(2,128)} %slot_ref.1) | copy-start | bytes 73732
  15.1 6.3 %collective-permute-start.2 = (f32[3,3072]{1,0:T(4,128)S(1)}, f32[3,3072]{1,0:T(4,128)S(1)}, u32[]{:S(2)}, u32[]{:S(2)}) collective-permute-start(f32[3,3072]{1,0:T(4,128)S(1)} %get-tuple-element.25), channel_id=1, source_target_pairs={{0,8},{16,24},{8,0},{24,16},{1,9},{17,25},{9,1},{25,17},{2,10},{18... | collective-permute-start | bytes 110600 | tf_op jit(solution)/shard_map/ppermute | solution.py:398
  17.0 6.9 %collective-permute-start.3 = (f32[3,3072]{1,0:T(4,128)S(1)}, f32[3,3072]{1,0:T(4,128)S(1)}, u32[]{:S(2)}, u32[]{:S(2)}) collective-permute-start(f32[3,3072]{1,0:T(4,128)S(1)} %get-tuple-element.26), channel_id=1, source_target_pairs={{8,16},{24,0},{16,8},{0,24},{9,17},{25,1},{17,9},{1,25},{10,18},{2... | collective-permute-start | bytes 110600 | tf_op jit(solution)/shard_map/ppermute | solution.py:398
